TPU v7x, 256 devices: a whole 4x4x8 slice. The times are simulated.
256 devices in a mesh: src: 8 (over x, y_hi), dst: 32 (over z, y_lo, core).
Axes of the slice: x: 4, y: 4 (y_hi: 2, y_lo: 2; y = y_hi * 2 + y_lo), z: 8, core: 2. Of those that a mesh axis runs over, the one named last changes fastest.
Arguments:
- edge_in: bfloat16 [1048576, 512], P(('src', 'dst')), may hold values from -6 to 6
- atom_in: bfloat16 [16384, 256], P(('dst', 'src')), may hold values from -6 to 6
- targets: int32 [1048576], P(('src', 'dst')), may hold values from 0 to 511
- reverse: int32 [1048576], P(('src', 'dst')), may hold values from 0 to 127, as said below
- counts: int32 [8, 32, 32], P('src', 'dst'), may hold values from 2 to 128, as said below
- w_in: bfloat16 [256, 512], replicated, may hold values from -0.375 to 0.375
- gains: float32 [2, 512], replicated, may hold values from 0.1 to 1.9
- w_layers: bfloat16 [2, 512, 512], replicated, may hold values from -0.25 to 0.25
- w_rev: bfloat16 [512, 512], replicated, may hold values from -0.25 to 0.25
- w_down: bfloat16 [512, 256], replicated, may hold values from -0.25 to 0.25
- w_atom: bfloat16 [256, 256], replicated, may hold values from -0.375 to 0.375
Outputs:
- edge_out: bfloat16 [1048576, 512], P(('src', 'dst'))
- atom_out: bfloat16 [16384, 256], P(('dst', 'src'))
Inputs may be any that keep to these rules, and one draw needn't show every extreme that they name: In every block k of tile (i, j), reverse maps the used slots one to one onto the used slots of block j of tile (i, k), and the two maps are inverse to each other; in block j of tile (i, j) it pairs used slots and is its own inverse. Unused slots map onto unused slots. Every count is even, and counts[i, j, k] equals counts[i, k, j].
All inputs are finite; a program needn't handle non-finite values.
Results may differ from a plain program's by a relative error of at most 0.014.
Values may be sent and summed in bfloat16 or wider, within the bound.
A program may use at most 128 MiB of HBM per device.

v0:
```python
import jax
import jax.numpy as jnp
from jax import lax
from jax.sharding import Mesh
from jax.sharding import PartitionSpec as P

SRC = ("src_0", "src_1")
SRC_DST = ("src_0", "src_1", "dst")
DST_SRC = ("dst", "src_0", "src_1")


def laid_out(pieces, dim):
    pieces = jnp.moveaxis(pieces, 0, dim)
    lengths = pieces.shape
    return pieces.reshape(*lengths[:dim], lengths[dim] * lengths[dim + 1], *lengths[dim + 2 :])


def from_everyone(shard, axis):
    length = lax.axis_size(axis)
    return lax.all_to_all(
        jnp.broadcast_to(shard[None], (length, *shard.shape)), axis, 0, 0, tiled=True
    )


def gathered_copies(shard, axis, dim):
    return laid_out(from_everyone(shard, axis), dim)


def sum_by_axis(terms, axes):
    so_far = terms.astype(jnp.bfloat16)
    for axis in axes:
        so_far = lax.psum_scatter(so_far, axis, scatter_dimension=0, tiled=True)
    return so_far.astype(jnp.float32)


def edge_layers(base, picked, gains, w_layers):
    state = base.astype(jnp.float32) + picked.astype(jnp.float32)
    for layer in range(w_layers.shape[0]):
        scale = lax.rsqrt(jnp.mean(state * state, axis=-1, keepdims=True) + 1e-06)
        normed = (state * scale * gains[layer]).astype(jnp.bfloat16)
        state = state + jax.nn.silu(
            jnp.dot(normed, w_layers[layer], preferred_element_type=jnp.float32)
        )
    return state


def on_device(
    edge_in, atom_in, targets, reverse, counts, w_in, gains, w_layers, w_rev, w_down, w_atom
):
    slots = edge_in.shape[0]
    blocks = counts.shape[2]
    width = slots // blocks
    place = jnp.arange(slots)
    owner = place // width
    used = place % width < jnp.repeat(counts.reshape(blocks), width)
    whole = gathered_copies(atom_in, SRC, 0)
    atom_proj = jnp.dot(whole, w_in, preferred_element_type=jnp.float32).astype(jnp.bfloat16)
    picked = jnp.take(atom_proj, targets, axis=0)
    source = owner * width + reverse
    state = edge_layers(edge_in, picked, gains, w_layers)
    sent = state.astype(jnp.bfloat16)
    arrived = lax.all_to_all(sent, "dst", split_axis=0, concat_axis=0, tiled=True)
    mirrored = jnp.take(arrived, source, axis=0)
    combined = jnp.where(
        used[:, None],
        state + jnp.dot(mirrored, w_rev, preferred_element_type=jnp.float32),
        jnp.float32(0.0),
    )
    edge_out = combined.astype(jnp.bfloat16)
    contrib = jnp.where(
        used[:, None],
        jnp.dot(edge_out, w_down, preferred_element_type=jnp.float32),
        jnp.float32(0.0),
    )
    count = atom_in.shape[0] * lax.axis_size(SRC)
    inside = (targets >= 0) & (targets < count)
    labels = jnp.where(inside, targets, count)
    summed = jax.ops.segment_sum(contrib, labels, num_segments=count + 1)
    agg = sum_by_axis(summed[:count], SRC)
    act = jax.nn.silu(0.3 * agg).astype(jnp.bfloat16)
    atom_out = (
        atom_in.astype(jnp.float32) + jnp.dot(act, w_atom, preferred_element_type=jnp.float32)
    ).astype(jnp.bfloat16)
    return (edge_out, atom_out)


def solution(mesh):
    torus = Mesh(mesh.devices.reshape(4, 2, mesh.shape["dst"]), ("src_0", "src_1", "dst"))
    in_specs = (
        P(SRC_DST, None),
        P(DST_SRC, None),
        P(SRC_DST),
        P(SRC_DST),
        P(SRC, "dst", None),
        P(),
        P(),
        P(),
        P(),
        P(),
        P(),
    )
    out_specs = (P(SRC_DST, None), P(DST_SRC, None))
    return jax.shard_map(
        on_device, mesh=torus, in_specs=in_specs, out_specs=out_specs, check_vma=False
    )
```

profile of v0, /device:TPU:32, one launch (start us, length us, event | category | flops | bytes accessed | tf_op | source)
XLA Modules:
  0.0 265.4 jit_solution(7653357958005642313)
XLA Ops:
  7.2 0.0 copy-start
  7.2 1.5 broadcast_in_dim.70
  8.7 6.9 %all-to-all-start = ((bf16[8,64,256]{2,1,0:T(8,128)(2,1)}), bf16[8,64,256]{2,1,0:T(8,128)(2,1)S(1)}, u32[]{:S(2)}, u32[]{:S(2)}) async-start(bf16[8,64,256]{2,1,0:T(8,128)(2,1)} %broadcast_in_dim.70), calls=%async_computation | async-start | bytes 524288 | tf_op jit(solution)/shard_map/all_to_all | solution.py:20
  15.6 0.7 compare_and_fusion.1
  16.4 0.8 fusion.31
  17.1 0.7 and_select_fusion
  17.9 6.5 %all-to-all-done = bf16[8,64,256]{2,1,0:T(8,128)(2,1)S(1)} async-done(((bf16[8,64,256]{2,1,0:T(8,128)(2,1)}), bf16[8,64,256]{2,1,0:T(8,128)(2,1)S(1)}, u32[]{:S(2)}, u32[]{:S(2)}) %all-to-all-start) | async-done | bytes 262176 | tf_op jit(solution)/shard_map/all_to_all | solution.py:20
  24.4 1.2 convolution_convert_fusion
  25.6 0.0 copy-start.8
  25.6 17.3 %gather_fusion = bf16[4096,512]{1,0:T(8,128)(2,1)} fusion(bf16[512,512]{1,0:T(8,128)(2,1)S(1)} %convolution_convert_fusion, s32[4096]{0:T(1024)S(1)} %get-tuple-element.3), kind=kCustom, calls=%fused_computation | custom fusion | bytes 8404992 | tf_op jit(solution)/shard_map/jit(_take)/gather | solution.py:58
  43.0 0.0 copy-start.1
  43.0 0.0 copy-start.3
  43.0 5.1 %multiply_reduce_fusion.1 = f32[4096]{0:T(1024)S(1)} fusion(bf16[4096,512]{1,0:T(8,128)(2,1)} %param.11, bf16[4096,512]{1,0:T(8,128)(2,1)} %gather_fusion, pred[4096]{0:T(1024)(128)(4,1)S(1)} %compare_and_fusion.1), kind=kLoop, calls=%fused_computation.9 | loop fusion | flops 12578816 | bytes 8409088 | tf_op jit(solution)/shard_map/reduce_sum | solution.py:39
  48.1 0.0 copy-done.8
  48.2 0.0 copy-done.1
  48.2 0.7 copy-done.3
  48.9 5.9 %multiply_reduce_fusion = (f32[4096]{0:T(1024)S(1)}, f32[4096,512]{1,0:T(8,128)S(1)}) fusion(bf16[2,512,512]{2,1,0:T(8,128)(2,1)S(1)} %copy-done.8, bf16[4096,512]{1,0:T(8,128)(2,1)S(1)} %copy-done.3, f32[512]{0:T(512)S(1)} %bitcast.27, f32[4096]{0:T(1024)S(1)} %add_rsqrt_fusion.1, bf16[4096,512]{1,0:T(8,128)(2,1)S(1)} %copy-done.1, ...), kind=kOutput, calls=%fused_computation.6 | convolution fusion | flops 2185228288 | bytes 25733120 | tf_op jit(solution)/shard_map/dot_general | solution.py:42
  54.8 7.2 %fusion.32 = (bf16[4096,512]{1,0:T(8,128)(2,1)}, f32[4096,512]{1,0:T(8,128)}) fusion(f32[4096,512]{1,0:T(8,128)S(1)} %get-tuple-element.7, bf16[2,512,512]{2,1,0:T(8,128)(2,1)S(1)} %copy-done.8, f32[512]{0:T(512)S(1)} %bitcast.26, f32[4096]{0:T(1024)S(1)} %add_rsqrt_fusion), kind=kOutput, calls=%fused_computation.62 | convolution fusion | flops 2166358016 | bytes 29902848 | tf_op jit(solution)/shard_map/dot_general | solution.py:42
  62.1 0.0 copy-start.5
  62.1 0.0 copy-start.7
  62.1 9.0 %all-to-all-start.1 = ((bf16[32,128,512]{2,1,0:T(8,128)(2,1)}), bf16[32,128,512]{2,1,0:T(8,128)(2,1)}, u32[]{:S(2)}, u32[]{:S(2)}) async-start(bf16[32,128,512]{2,1,0:T(8,128)(2,1)} %bitcast.24), calls=%async_computation.1 | async-start | bytes 8388608 | tf_op jit(solution)/shard_map/all_to_all | solution.py:62
  71.1 0.2 reduce-scatter.3.cloned.1.call-start
  71.3 0.0 copy-done.5
  71.3 0.0 copy-done.7
  71.3 0.1 fusion.18
  71.4 95.2 %all-to-all-done.1 = bf16[32,128,512]{2,1,0:T(8,128)(2,1)} async-done(((bf16[32,128,512]{2,1,0:T(8,128)(2,1)}), bf16[32,128,512]{2,1,0:T(8,128)(2,1)}, u32[]{:S(2)}, u32[]{:S(2)}) %all-to-all-start.1) | async-done | bytes 4194336 | tf_op jit(solution)/shard_map/all_to_all | solution.py:62
  166.6 20.2 %gather_fusion.1 = bf16[4096,512]{1,0:T(8,128)(2,1)} fusion(bf16[4096,512]{1,0:T(8,128)(2,1)} %bitcast.8, s32[4096]{0:T(1024)S(1)} %broadcast_clamp_fusion), kind=kCustom, calls=%fused_computation.1 | custom fusion | bytes 8404992 | tf_op jit(solution)/shard_map/jit(_take)/gather | solution.py:63
  186.8 0.0 copy-done
  186.8 0.0 copy-start.4
  186.8 6.0 %select_convert_fusion = bf16[4096,512]{1,0:T(8,128)(2,1)S(1)} fusion(f32[4096,512]{1,0:T(8,128)} %get-tuple-element.9, bf16[512,512]{1,0:T(8,128)(2,1)S(1)} %copy-done, bf16[4096,512]{1,0:T(8,128)(2,1)} %gather_fusion.1, pred[4096]{0:T(1024)(128)(4,1)S(1)} %get-tuple-element.11, pred[4096]{0:T(1024)(128)(4,1)S(1)} %get-tuple-element.10), kind=kOutput, calls=%fused_computation.3 | convolution fusion | flops 2155872256 | bytes 17309696 | tf_op jit(solution)/shard_map/dot_general | solution.py:66
  192.8 0.0 copy-done.4
  192.8 0.0 copy-start.2
  192.8 0.0 copy-start.6
  192.8 0.0 copy-start.9
  192.9 4.4 %convolution_select_fusion = f32[4096,256]{1,0:T(8,128)} fusion(bf16[4096,512]{1,0:T(8,128)(2,1)S(1)} %select_convert_fusion, bf16[512,256]{1,0:T(8,128)(2,1)S(1)} %copy-done.4, pred[4096]{0:T(1024)(128)(4,1)S(1)} %get-tuple-element.10), kind=kOutput, calls=%fused_computation.11 | convolution fusion | flops 1074790400 | bytes 8654848 | tf_op jit(solution)/shard_map/dot_general | solution.py:72
  197.2 0.0 copy-done.2
  197.2 22.9 %scatter_custom_fusion = f32[513,256]{1,0:T(8,128)S(1)} fusion(s32[4096]{0:T(1024)S(1)} %get-tuple-element.2, f32[4096,256]{1,0:T(8,128)} %convolution_select_fusion, f32[]{:T(128)} %constant.71.clone.1), kind=kCustom, calls=%fused_computation.30 | custom fusion | flops 1048576 | bytes 525824 | tf_op jit(solution)/shard_map/scatter-add | solution.py:78
  220.2 0.7 slice.35
  220.9 0.0 reduce-scatter.3.cloned.1.call-update
  220.9 0.0 reduce-scatter.5.cloned.1.call-start
  221.0 17.2 %reduce-scatter.3.cloned.1.call-done = bf16[128,256]{1,0:T(8,128)(2,1)} async-done(((bf16[512,256]{1,0:T(8,128)(2,1)}), bf16[128,256]{1,0:T(8,128)(2,1)}) %reduce-scatter.3.cloned.1.call-update) | async-done | bytes 65552 | tf_op jit(solution)/shard_map/reduce_scatter | solution.py:32
  238.2 0.0 reduce-scatter.5.cloned.1.call-update
  238.2 18.8 %reduce-scatter.5.cloned.1.call-done = bf16[64,256]{1,0:T(8,128)(2,1)} async-done(((bf16[128,256]{1,0:T(8,128)(2,1)}), bf16[64,256]{1,0:T(8,128)(2,1)}) %reduce-scatter.5.cloned.1.call-update) | async-done | bytes 32784 | tf_op jit(solution)/shard_map/reduce_scatter | solution.py:32
  257.0 0.0 copy-done.6
  257.0 0.0 copy-done.9
  257.0 1.5 fusion.9
  (3 shorter events, 0.0 us)
Async XLA Ops:
  7.2 179.6 %copy-start = (bf16[512,512]{1,0:T(8,128)(2,1)S(1)}, bf16[512,512]{1,0:T(8,128)(2,1)}, u32[]{:S(2)}) copy-start(bf16[512,512]{1,0:T(8,128)(2,1)} %param.19) | copy-start | bytes 1572868
  8.7 15.6 %all-to-all-start = ((bf16[8,64,256]{2,1,0:T(8,128)(2,1)}), bf16[8,64,256]{2,1,0:T(8,128)(2,1)S(1)}, u32[]{:S(2)}, u32[]{:S(2)}) async-start(bf16[8,64,256]{2,1,0:T(8,128)(2,1)} %broadcast_in_dim.70), calls=%async_computation | async-start | bytes 524288 | tf_op jit(solution)/shard_map/all_to_all | solution.py:20
  25.6 22.5 %copy-start.8 = (bf16[2,512,512]{2,1,0:T(8,128)(2,1)S(1)}, bf16[2,512,512]{2,1,0:T(8,128)(2,1)}, u32[]{:S(2)}) copy-start(bf16[2,512,512]{2,1,0:T(8,128)(2,1)} %param.18) | copy-start | bytes 3145732
  43.0 5.2 %copy-start.1 = (bf16[4096,512]{1,0:T(8,128)(2,1)S(1)}, bf16[4096,512]{1,0:T(8,128)(2,1)}, u32[]{:S(2)}) copy-start(bf16[4096,512]{1,0:T(8,128)(2,1)} %gather_fusion) | copy-start | bytes 12582916
  43.0 5.9 %copy-start.3 = (bf16[4096,512]{1,0:T(8,128)(2,1)S(1)}, bf16[4096,512]{1,0:T(8,128)(2,1)}, u32[]{:S(2)}) copy-start(bf16[4096,512]{1,0:T(8,128)(2,1)} %param.11) | copy-start | bytes 12582916
  62.1 9.3 %copy-start.5 = (s32[4096]{0:T(1024)S(1)}, s32[4096]{0:T(1024)}, u32[]{:S(2)}) copy-start(s32[4096]{0:T(1024)} %param.14) | copy-start | bytes 49156
  62.1 9.3 %copy-start.7 = (s32[1,1,32]{2,1,0:T(1,128)S(1)}, s32[1,1,32]{2,1,0:T(1,128)}, u32[]{:S(2)}) copy-start(s32[1,1,32]{2,1,0:T(1,128)} %param.15) | copy-start | bytes 388
  62.1 104.6 %all-to-all-start.1 = ((bf16[32,128,512]{2,1,0:T(8,128)(2,1)}), bf16[32,128,512]{2,1,0:T(8,128)(2,1)}, u32[]{:S(2)}, u32[]{:S(2)}) async-start(bf16[32,128,512]{2,1,0:T(8,128)(2,1)} %bitcast.24), calls=%async_computation.1 | async-start | bytes 8388608 | tf_op jit(solution)/shard_map/all_to_all | solution.py:62
  71.1 167.1 %reduce-scatter.3.cloned.1.call-start = ((), (), s32[]{:S(2)}) async-start(), calls=%async_computation.4 | async-start | bytes 327680 | tf_op jit(solution)/shard_map/reduce_scatter | solution.py:32
  186.8 6.0 %copy-start.4 = (bf16[512,256]{1,0:T(8,128)(2,1)S(1)}, bf16[512,256]{1,0:T(8,128)(2,1)}, u32[]{:S(2)}) copy-start(bf16[512,256]{1,0:T(8,128)(2,1)} %param.20) | copy-start | bytes 786436
  192.8 4.4 %copy-start.2 = (bf16[4096,512]{1,0:T(8,128)(2,1)}, bf16[4096,512]{1,0:T(8,128)(2,1)S(1)}, u32[]{:S(2)}) copy-start(bf16[4096,512]{1,0:T(8,128)(2,1)S(1)} %select_convert_fusion) | copy-start | bytes 12582916
  192.8 64.2 %copy-start.6 = (bf16[64,256]{1,0:T(8,128)(2,1)S(1)}, bf16[64,256]{1,0:T(8,128)(2,1)}, u32[]{:S(2)}) copy-start(bf16[64,256]{1,0:T(8,128)(2,1)} %param.12) | copy-start | bytes 98308
  192.8 64.2 %copy-start.9 = (bf16[256,256]{1,0:T(8,128)(2,1)S(1)}, bf16[256,256]{1,0:T(8,128)(2,1)}, u32[]{:S(2)}) copy-start(bf16[256,256]{1,0:T(8,128)(2,1)} %param.21) | copy-start | bytes 393220
  220.9 36.1 %reduce-scatter.5.cloned.1.call-start = ((), (), s32[]{:S(2)}) async-start(), calls=%async_computation.5 | async-start | bytes 98304 | tf_op jit(solution)/shard_map/reduce_scatter | solution.py:32
Sparse Core Ops, SparseCore 0:
  221.1 17.0 reduce-scatter.2
  240.8 16.2 reduce-scatter.4
where the time goes:
time: 267 us; the launch traced here: 265 us
  waiting for transfers between devices  138 us (52%)
  local copies, waits for them, and re-layouts  41.3 us (15%)
  other arithmetic  29.7 us (11%)
  matrix products  26.3 us (10%)
  starting transfers between devices  16.2 us (6%)
  between operations  14.2 us (5%)
    all_to_all x1, waiting for transfers between devices, on_device(): lax.all_to_all(sent, 'dst', split_axis=0, concat_axis=0, tiled=True)  95.2 us
    reduce_scatter x2, waiting for transfers between devices, sum_by_axis(): so_far = lax.psum_scatter(so_far, axis, scatter_dimension=0, tiled=True)  36 us
    scatter-add x1, other arithmetic, on_device(): summed = jax.ops.segment_sum(contrib, labels, num_segments=count + 1)  22.9 us
    gather x1, local copies, waits for them, and re-layouts, on_device(): mirrored = jnp.take(arrived, source, axis=0)  20.2 us
    gather x1, local copies, waits for them, and re-layouts, on_device(): picked = jnp.take(atom_proj, targets, axis=0)  17.3 us
    dot_general x2, matrix products, edge_layers(): jnp.dot(normed, w_layers[layer], preferred_element_type=jnp.float32)  13.1 us
    all_to_all x1, starting transfers between devices, on_device(): lax.all_to_all(sent, 'dst', split_axis=0, concat_axis=0, tiled=True)  9.04 us
    all_to_all x1, starting transfers between devices, from_everyone(): lax.all_to_all(jnp.broadcast_to(shard[None], (length, *shard.shape)), axi...  6.93 us
  transfers between devices with their start and end apart: 4, of which 4 were waited for; matrix products, arithmetic and copies ran while one was open for 1% of the time, Pallas kernels for 0%

commit v1 on v0

v1 whole, which is shorter than its diff:
```python
import functools

import jax
import jax.numpy as jnp
from jax import lax
from jax.experimental import pallas as pl
from jax.experimental.pallas import tpu as pltpu
from jax.sharding import PartitionSpec as P

MESH = pl.DeviceIdType.MESH
RB = 128
PLANE = 4


def silu(v):
    half = 0.5 * v
    return half + half * jnp.tanh(half)


def kernel(
    n_src, n_dst,
    edge_ref, atom_ref, targ_ref, rev_ref, cnt_ref, w_in_ref, gains_ref, w_lay_ref, w_rev_ref, w_down_ref, w_atom_ref,
    edge_out_ref, atom_out_ref,
    edges, xs, send, recv, atoms, proj, w_in, w_lay, w_rev, w_down, w_atom, seg, part, parts,
    in_sem, w_sem, at_send, at_recv, send_sem, recv_sem, out_sem, pt_send, pt_recv,
):
    planes = n_dst // PLANE
    width = edges.shape[1]
    layers = w_lay.shape[0]
    n_atoms = proj.shape[0]
    chunk = PLANE * RB
    row = lax.axis_index("src")
    me = lax.axis_index("dst")
    z = me // PLANE

    barrier = pltpu.get_barrier_semaphore()

    @pl.loop(1, n_src)
    def _(d):
        pl.semaphore_signal(barrier, inc=1, device_id={"src": lax.rem(row + d, n_src)}, device_id_type=MESH)

    @pl.loop(1, n_dst)
    def _(d):
        pl.semaphore_signal(barrier, inc=1, device_id={"dst": lax.rem(me + d, n_dst)}, device_id_type=MESH)

    def out_plane(n):
        dz = jnp.where(n % 2 == 0, planes // 2 + n // 2, planes // 2 - 1 - n // 2)
        return lax.rem(z + dz, planes)

    def in_plane(n):
        dz = jnp.where(n % 2 == 0, planes // 2 - n // 2, planes // 2 + 1 + n // 2)
        return lax.rem(z + dz, planes)

    def rows_of(zp):
        return pl.ds(pl.multiple_of(zp * chunk, chunk), chunk)

    def edge_load(zp):
        return pltpu.make_async_copy(edge_ref.at[rows_of(zp)], edges.at[rows_of(zp)], in_sem.at[zp])

    weight_loads = [
        pltpu.make_async_copy(src, dst, w_sem.at[i])
        for i, (src, dst) in enumerate(
            [(w_in_ref, w_in), (w_lay_ref, w_lay), (w_rev_ref, w_rev), (w_down_ref, w_down), (w_atom_ref, w_atom)]
        )
    ]
    own_atoms = pltpu.make_async_copy(atom_ref, atoms.at[row], w_sem.at[5])
    own_atoms.start()
    weight_loads[0].start()
    weight_loads[1].start()

    @pl.loop(0, planes)
    def _(n):
        edge_load(out_plane(n)).start()

    for load in weight_loads[2:]:
        load.start()
    seg[...] = jnp.zeros_like(seg)

    pl.semaphore_wait(barrier, n_src + n_dst - 2)

    def atom_copy(d):
        return pltpu.make_async_remote_copy(
            src_ref=atom_ref, dst_ref=atoms.at[row], send_sem=at_send.at[d], recv_sem=at_recv.at[d],
            device_id={"src": lax.rem(row + d, n_src)}, device_id_type=MESH,
        )

    @pl.loop(1, n_src)
    def _(d):
        atom_copy(d).start()

    weight_loads[0].wait()
    weight_loads[1].wait()
    own_atoms.wait()

    @pl.loop(1, n_src)
    def _(d):
        atom_copy(d).wait()

    whole = atoms[...].reshape(n_atoms, atoms.shape[2])
    proj[...] = jnp.dot(whole, w_in[...], preferred_element_type=jnp.float32).astype(jnp.bfloat16)

    def block_copy(k):
        return pltpu.make_async_remote_copy(
            src_ref=send.at[k], dst_ref=recv.at[me], send_sem=send_sem.at[k], recv_sem=recv_sem.at[me],
            device_id={"dst": k}, device_id_type=MESH,
        )

    def arrival(k):
        return pltpu.make_async_remote_copy(
            src_ref=send.at[k], dst_ref=recv.at[k], send_sem=send_sem.at[k], recv_sem=recv_sem.at[k],
            device_id={"dst": k}, device_id_type=MESH,
        )

    def own_copy():
        return pltpu.make_async_copy(send.at[me], recv.at[me], recv_sem.at[me])

    @pl.loop(0, planes)
    def _(n):
        zp = out_plane(n)
        edge_load(zp).wait()
        hot = []
        targ = targ_ref[zp]
        for q in range(PLANE):
            col = jnp.broadcast_to(targ[q : q + 1, :], (RB, RB)).T
            lane = lax.broadcasted_iota(jnp.int32, (RB, RB), 1)
            hot.append(
                jnp.concatenate(
                    [(col == lane + p * RB).astype(jnp.float32).astype(jnp.bfloat16) for p in range(n_atoms // RB)], axis=1
                )
            )
        picked = jnp.dot(jnp.concatenate(hot, axis=0), proj[...], preferred_element_type=jnp.float32)
        x = edges[rows_of(zp), :].astype(jnp.float32) + picked
        for layer in range(layers):
            scale = lax.rsqrt(jnp.mean(x * x, axis=-1, keepdims=True) + 1e-6)
            normed = (x * scale * gains_ref[layer : layer + 1, :]).astype(jnp.bfloat16)
            x = x + silu(jnp.dot(normed, w_lay[layer], preferred_element_type=jnp.float32))
        xs[rows_of(zp), :] = x
        sent = x.astype(jnp.bfloat16)
        rev = rev_ref[zp]
        for q in range(PLANE):
            k = zp * PLANE + q
            sub = lax.broadcasted_iota(jnp.int32, (RB, RB), 0)
            perm = (sub == rev[q : q + 1, :]).astype(jnp.float32).astype(jnp.bfloat16)
            moved = jnp.dot(perm, sent[q * RB : (q + 1) * RB, :], preferred_element_type=jnp.float32)
            send[k] = moved.astype(jnp.bfloat16)

            @pl.when(k != me)
            def _():
                block_copy(k).start()

            @pl.when(k == me)
            def _():
                own_copy().start()

    for load in weight_loads[2:]:
        load.wait()

    def edge_store(zp):
        return pltpu.make_async_copy(edges.at[rows_of(zp)], edge_out_ref.at[rows_of(zp)], out_sem.at[zp])

    @pl.loop(0, planes)
    def _(n):
        zp = in_plane(n)
        for q in range(PLANE):
            k = zp * PLANE + q

            @pl.when(k != me)
            def _():
                arrival(k).wait_recv()

            @pl.when(k == me)
            def _():
                own_copy().wait()

        came = recv[pl.ds(zp * PLANE, PLANE)].reshape(chunk, width)
        total = xs[rows_of(zp), :] + jnp.dot(came, w_rev[...], preferred_element_type=jnp.float32)
        kept = []
        for q in range(PLANE):
            slot = lax.broadcasted_iota(jnp.int32, (RB, width), 0)
            kept.append(jnp.where(slot < cnt_ref[zp * PLANE + q], total[q * RB : (q + 1) * RB, :], 0.0))
        result = jnp.concatenate(kept, axis=0).astype(jnp.bfloat16)
        edges[rows_of(zp), :] = result
        edge_store(zp).start()
        targ = targ_ref[zp]
        sub = lax.broadcasted_iota(jnp.int32, (n_atoms, RB), 0)
        hot = jnp.concatenate(
            [(sub == targ[q : q + 1, :]).astype(jnp.float32).astype(jnp.bfloat16) for q in range(PLANE)], axis=1
        )
        seg[...] += jnp.dot(hot, result, preferred_element_type=jnp.float32)

    down = jnp.dot(seg[...].astype(jnp.bfloat16), w_down[...], preferred_element_type=jnp.float32)
    part[...] = down.astype(jnp.bfloat16).reshape(part.shape)

    def part_copy(d):
        to = lax.rem(row + d, n_src)
        return pltpu.make_async_remote_copy(
            src_ref=part.at[to], dst_ref=parts.at[d], send_sem=pt_send.at[d], recv_sem=pt_recv.at[d],
            device_id={"src": to}, device_id_type=MESH,
        )

    @pl.loop(1, n_src)
    def _(d):
        part_copy(d).start()

    agg = part[row].astype(jnp.float32)

    @pl.loop(1, n_src)
    def _(d):
        part_copy(d).wait()

    for d in range(1, n_src):
        agg = agg + parts[d].astype(jnp.float32)
    act = silu(0.3 * agg).astype(jnp.bfloat16)
    update = jnp.dot(act, w_atom[...], preferred_element_type=jnp.float32)
    atom_out_ref[...] = (atoms[row].astype(jnp.float32) + update).astype(jnp.bfloat16)

    @pl.loop(0, n_dst)
    def _(k):
        @pl.when(k != me)
        def _():
            arrival(k).wait_send()

    @pl.loop(0, planes)
    def _(n):
        edge_store(n).wait()


def solution(mesh):
    n_src, n_dst = mesh.shape["src"], mesh.shape["dst"]
    planes = n_dst // PLANE

    def on_device(edge_in, atom_in, targets, reverse, counts, w_in, gains, w_layers, w_rev, w_down, w_atom):
        slots, width = edge_in.shape
        own, depth = atom_in.shape
        n_atoms = own * n_src
        bf16, f32 = jnp.bfloat16, jnp.float32
        anywhere = pl.BlockSpec(memory_space=pl.ANY)
        vmem = pl.BlockSpec(memory_space=pltpu.VMEM)
        smem = pl.BlockSpec(memory_space=pltpu.SMEM)
        dma = pltpu.SemaphoreType.DMA
        return pl.pallas_call(
            functools.partial(kernel, n_src, n_dst),
            out_shape=(
                jax.ShapeDtypeStruct(edge_in.shape, bf16),
                jax.ShapeDtypeStruct(atom_in.shape, bf16),
            ),
            in_specs=[anywhere, anywhere, vmem, vmem, smem, anywhere, vmem] + [anywhere] * 4,
            out_specs=(anywhere, vmem),
            scratch_shapes=[
                pltpu.VMEM((slots, width), bf16),
                pltpu.VMEM((slots, width), f32),
                pltpu.VMEM((n_dst, RB, width), bf16),
                pltpu.VMEM((n_dst, RB, width), bf16),
                pltpu.VMEM((n_src, own, depth), bf16),
                pltpu.VMEM((n_atoms, width), bf16),
                pltpu.VMEM(w_in.shape, bf16),
                pltpu.VMEM(w_layers.shape, bf16),
                pltpu.VMEM(w_rev.shape, bf16),
                pltpu.VMEM(w_down.shape, bf16),
                pltpu.VMEM(w_atom.shape, bf16),
                pltpu.VMEM((n_atoms, width), f32),
                pltpu.VMEM((n_src, own, depth), bf16),
                pltpu.VMEM((n_src, own, depth), bf16),
                dma((planes,)),
                dma((6,)),
                dma((n_src,)),
                dma((n_src,)),
                dma((n_dst,)),
                dma((n_dst,)),
                dma((planes,)),
                dma((n_src,)),
                dma((n_src,)),
            ],
            compiler_params=pltpu.CompilerParams(
                collective_id=0, has_side_effects=True, vmem_limit_bytes=56 * 2**20
            ),
        )(
            edge_in, atom_in, targets.reshape(planes, PLANE, RB), reverse.reshape(planes, PLANE, RB), counts.reshape(n_dst),
            w_in, gains, w_layers, w_rev, w_down, w_atom,
        )

    both = ("src", "dst")
    in_specs = (
        P(both, None), P(("dst", "src"), None), P(both), P(both), P("src", "dst", None),
        P(), P(), P(), P(), P(), P(),
    )
    out_specs = (P(both, None), P(("dst", "src"), None))
    return jax.shard_map(on_device, mesh=mesh, in_specs=in_specs, out_specs=out_specs, check_vma=False)
```

time: 267 us -> 133 us (0.50)
  the two profiles are of different devices: /device:TPU:32 before, /device:TPU:57 now
where the time goes in v1:
time: 133 us
  Pallas kernels  127 us (95%)
  local copies, waits for them, and re-layouts  5.09 us (4%)
    pallas_call x1, Pallas kernels, on_device(): pl.pallas_call(functools.partial(kernel, n_src, n_dst), out_shape=(jax.Sh...  127 us
    unnamed x4, local copies, waits for them, and re-layouts  5.09 us

profile of v1, /device:TPU:57, one launch (start us, length us, event | category | flops | bytes accessed | tf_op | source)
XLA Modules:
  0.0 132.9 jit_solution(6048360496845593917)
XLA Ops:
  0.6 127.1 %shard_map.122 = (bf16[4096,512]{1,0:T(8,128)(2,1)}, bf16[64,256]{1,0:T(8,128)(2,1)}) custom-call(bf16[4096,512]{1,0:T(8,128)(2,1)} %edge_ref.1, bf16[64,256]{1,0:T(8,128)(2,1)} %atom_ref.1, s32[8,4,128]{2,1,0:T(4,128)} %bitcast.3, s32[8,4,128]{2,1,0:T(4,128)} %bitcast.4, s32[32]{0:T(128)} %bitcast.5, bf16[256,512]{1,0:T(8,128)(2,1)} %w_in_ref.1, ...), custom_call_target="tpu_custom_call" | custom-call | tf_op jit(solution)/shard_map/pallas_call | solution.py:241
  127.8 0.0 copy-start
  127.8 4.5 %copy.15 = bf16[4096,512]{1,0:T(8,128)(2,1)} copy(bf16[4096,512]{1,0:T(8,128)(2,1)} %get-tuple-element.4) | data formatting | bytes 8388608
  132.2 0.0 copy-done
  132.2 0.6 copy.16
Async XLA Ops:
  127.8 4.5 %copy-start = (bf16[64,256]{1,0:T(8,128)(2,1)S(1)}, bf16[64,256]{1,0:T(8,128)(2,1)}, u32[]{:S(2)}) copy-start(bf16[64,256]{1,0:T(8,128)(2,1)} %get-tuple-element.5) | copy-start | bytes 98308

commit v2 on v1

v2 whole, which is shorter than its diff:
```python
import functools

import jax
import jax.numpy as jnp
from jax import lax
from jax.experimental import pallas as pl
from jax.experimental.pallas import tpu as pltpu
from jax.sharding import PartitionSpec as P

MESH = pl.DeviceIdType.MESH
RB = 128
PLANE = 4
AHEAD = 2
BEHIND = 2
VMEM_MIB = 54


def silu(v):
    half = 0.5 * v
    return half + half * jnp.tanh(half)


def far_peer(row, d, way, n_src):
    chips = n_src // 2
    same = d // (chips + 1)
    at = d - 1 - same * chips
    dx = jnp.where(at == chips - 1, 0, 1 + lax.rem(at + chips // 2 - 1, chips - 1))
    return lax.rem(row // 2 + way * dx + chips, chips) * 2 + lax.rem(row + 1 - same, 2)


def kernel(
    n_src, n_dst,
    edge_ref, atom_ref, targ_ref, rev_ref, cnt_ref, w_in_ref, gains_ref, w_lay_ref, w_rev_ref, w_down_ref, w_atom_ref,
    edge_out_ref, atom_out_ref,
    edges, xs, send, recv, atoms, proj, targ, rev, cnt, gains, w_in, w_lay, w_rev, w_down, w_atom, seg, part, parts,
    in_sem, w_sem, at_send, at_recv, send_sem, recv_sem, pt_send, pt_recv,
):
    planes = n_dst // PLANE
    width = edges.shape[1]
    layers = w_lay.shape[0]
    n_atoms = proj.shape[0]
    row = lax.axis_index("src")
    me = lax.axis_index("dst")
    z, y, c = me // PLANE, lax.rem(me // 2, 2), lax.rem(me, 2)

    barrier = pltpu.get_barrier_semaphore()

    @pl.loop(1, n_src)
    def _(d):
        pl.semaphore_signal(barrier, inc=1, device_id={"src": lax.rem(row + d, n_src)}, device_id_type=MESH)

    @pl.loop(1, n_dst)
    def _(d):
        pl.semaphore_signal(barrier, inc=1, device_id={"dst": lax.rem(me + d, n_dst)}, device_id_type=MESH)

    def partner(n, way):
        r, i = n // PLANE, lax.rem(n, PLANE)
        dz = planes // 2 * lax.rem(r + i, 2) + lax.rem(r // 2 + i + 1, planes // 2)
        py = lax.rem(y + i, 2)
        pc = lax.rem(c + (i + 1) // 2, 2)
        return lax.rem(z + way * dz + planes, planes) * PLANE + py * 2 + pc

    def rows_of(k):
        return pl.ds(pl.multiple_of(k * RB, RB), RB)

    def edge_load(k):
        return pltpu.make_async_copy(edge_ref.at[rows_of(k)], edges.at[rows_of(k)], in_sem.at[k])

    loads = [
        pltpu.make_async_copy(src, dst, w_sem.at[i])
        for i, (src, dst) in enumerate(
            [
                (atom_ref, atoms.at[row]), (w_in_ref, w_in), (targ_ref, targ), (gains_ref, gains), (w_lay_ref, w_lay),
                (rev_ref, rev), (w_rev_ref, w_rev), (cnt_ref, cnt), (w_down_ref, w_down), (w_atom_ref, w_atom),
            ]
        )
    ]
    for load in loads[:6]:
        load.start()

    @pl.loop(0, n_dst)
    def _(n):
        edge_load(partner(n, 1)).start()

    for load in loads[6:]:
        load.start()
    seg[...] = jnp.zeros_like(seg)
    loads[0].wait()
    pl.semaphore_wait(barrier, n_src + n_dst - 2)

    def atom_copy(d):
        return pltpu.make_async_remote_copy(
            src_ref=atoms.at[row], dst_ref=atoms.at[row], send_sem=at_send.at[d], recv_sem=at_recv.at[d],
            device_id={"src": far_peer(row, d, 1, n_src)}, device_id_type=MESH,
        )

    def atom_arrival(d):
        sender = far_peer(row, d, -1, n_src)
        return pltpu.make_async_remote_copy(
            src_ref=atoms.at[row], dst_ref=atoms.at[sender], send_sem=at_send.at[d], recv_sem=at_recv.at[d],
            device_id={"src": sender}, device_id_type=MESH,
        )

    @pl.loop(1, n_src)
    def _(d):
        atom_copy(d).start()

    for load in loads[1:6]:
        load.wait()

    @pl.loop(1, n_src)
    def _(d):
        atom_arrival(d).wait_recv()

    @pl.loop(1, n_src)
    def _(d):
        atom_copy(d).wait_send()

    whole = atoms[...].reshape(n_atoms, atoms.shape[2])
    proj[...] = jnp.dot(whole, w_in[...], preferred_element_type=jnp.float32).astype(jnp.bfloat16)

    def block_copy(k):
        return pltpu.make_async_remote_copy(
            src_ref=send.at[k], dst_ref=recv.at[me], send_sem=send_sem.at[k], recv_sem=recv_sem.at[me],
            device_id={"dst": k}, device_id_type=MESH,
        )

    def arrival(k):
        return pltpu.make_async_remote_copy(
            src_ref=send.at[k], dst_ref=recv.at[k], send_sem=send_sem.at[k], recv_sem=recv_sem.at[k],
            device_id={"dst": k}, device_id_type=MESH,
        )

    def own_copy():
        return pltpu.make_async_copy(send.at[me], recv.at[me], recv_sem.at[me])

    @pl.loop(0, n_dst // AHEAD)
    def _(step):
        ks = [partner(step * AHEAD + g, 1) for g in range(AHEAD)]
        hot, base = [], []
        for k in ks:
            edge_load(k).wait()
            base.append(edges[rows_of(k), :].astype(jnp.float32))
            col = jnp.broadcast_to(targ[k], (RB, RB)).T
            lane = lax.broadcasted_iota(jnp.int32, (RB, RB), 1)
            hot.append(
                jnp.concatenate(
                    [(col == lane + p * RB).astype(jnp.float32).astype(jnp.bfloat16) for p in range(n_atoms // RB)], axis=1
                )
            )
        picked = jnp.dot(jnp.concatenate(hot, axis=0), proj[...], preferred_element_type=jnp.float32)
        x = jnp.concatenate(base, axis=0) + picked
        for layer in range(layers):
            scale = lax.rsqrt(jnp.mean(x * x, axis=-1, keepdims=True) + 1e-6)
            normed = (x * scale * gains[layer : layer + 1, :]).astype(jnp.bfloat16)
            x = x + silu(jnp.dot(normed, w_lay[layer], preferred_element_type=jnp.float32))
        sent = x.astype(jnp.bfloat16)
        for g, k in enumerate(ks):
            xs[rows_of(k), :] = x[g * RB : (g + 1) * RB, :]
            sub = lax.broadcasted_iota(jnp.int32, (RB, RB), 0)
            perm = (sub == rev[k]).astype(jnp.float32).astype(jnp.bfloat16)
            moved = jnp.dot(perm, sent[g * RB : (g + 1) * RB, :], preferred_element_type=jnp.float32)
            send[k] = moved.astype(jnp.bfloat16)

            @pl.when(k != me)
            def _():
                block_copy(k).start()

            @pl.when(k == me)
            def _():
                own_copy().start()

    for load in loads[6:]:
        load.wait()

    @pl.loop(0, n_dst // BEHIND)
    def _(step):
        ks = [partner(step * BEHIND + g, -1) for g in range(BEHIND)]
        for k in ks:

            @pl.when(k != me)
            def _():
                arrival(k).wait_recv()

            @pl.when(k == me)
            def _():
                own_copy().wait()

        came = jnp.concatenate([recv[k] for k in ks], axis=0)
        message = jnp.dot(came, w_rev[...], preferred_element_type=jnp.float32)
        kept, hot = [], []
        for g, k in enumerate(ks):
            slot = lax.broadcasted_iota(jnp.int32, (RB, width), 0)
            total = xs[rows_of(k), :] + message[g * RB : (g + 1) * RB, :]
            result = jnp.where(slot < cnt[k], total, 0.0).astype(jnp.bfloat16)
            edge_out_ref[rows_of(k), :] = result
            kept.append(result)
            sub = lax.broadcasted_iota(jnp.int32, (n_atoms, RB), 0)
            hot.append((sub == targ[k]).astype(jnp.float32).astype(jnp.bfloat16))
        seg[...] += jnp.dot(
            jnp.concatenate(hot, axis=1), jnp.concatenate(kept, axis=0), preferred_element_type=jnp.float32
        )

    down = jnp.dot(seg[...].astype(jnp.bfloat16), w_down[...], preferred_element_type=jnp.float32)
    part[...] = down.astype(jnp.bfloat16).reshape(part.shape)

    def part_copy(d):
        to = far_peer(row, d, 1, n_src)
        return pltpu.make_async_remote_copy(
            src_ref=part.at[to], dst_ref=parts.at[d], send_sem=pt_send.at[d], recv_sem=pt_recv.at[d],
            device_id={"src": to}, device_id_type=MESH,
        )

    @pl.loop(1, n_src)
    def _(d):
        part_copy(d).start()

    agg = part[row].astype(jnp.float32)

    @pl.loop(1, n_src)
    def _(d):
        part_copy(d).wait()

    for d in range(1, n_src):
        agg = agg + parts[d].astype(jnp.float32)
    act = silu(0.3 * agg).astype(jnp.bfloat16)
    update = jnp.dot(act, w_atom[...], preferred_element_type=jnp.float32)
    atom_out_ref[...] = (atoms[row].astype(jnp.float32) + update).astype(jnp.bfloat16)

    @pl.loop(0, n_dst)
    def _(k):
        @pl.when(k != me)
        def _():
            arrival(k).wait_send()


def solution(mesh):
    n_src, n_dst = mesh.shape["src"], mesh.shape["dst"]

    def on_device(edge_in, atom_in, targets, reverse, counts, w_in, gains, w_layers, w_rev, w_down, w_atom):
        slots, width = edge_in.shape
        own, depth = atom_in.shape
        n_atoms = own * n_src
        bf16, f32 = jnp.bfloat16, jnp.float32
        hbm = pl.BlockSpec(memory_space=pltpu.HBM)
        vmem = pl.BlockSpec(memory_space=pltpu.VMEM)
        dma = pltpu.SemaphoreType.DMA
        return pl.pallas_call(
            functools.partial(kernel, n_src, n_dst),
            out_shape=(
                pltpu.VMEM(edge_in.shape, bf16),
                pltpu.VMEM(atom_in.shape, bf16),
            ),
            in_specs=[hbm] * 11,
            out_specs=(vmem, vmem),
            scratch_shapes=[
                pltpu.VMEM((slots, width), bf16),
                pltpu.VMEM((slots, width), f32),
                pltpu.VMEM((n_dst, RB, width), bf16),
                pltpu.VMEM((n_dst, RB, width), bf16),
                pltpu.VMEM((n_src, own, depth), bf16),
                pltpu.VMEM((n_atoms, width), bf16),
                pltpu.VMEM((n_dst, 1, RB), jnp.int32),
                pltpu.VMEM((n_dst, 1, RB), jnp.int32),
                pltpu.SMEM((n_dst,), jnp.int32),
                pltpu.VMEM(gains.shape, f32),
                pltpu.VMEM(w_in.shape, bf16),
                pltpu.VMEM(w_layers.shape, bf16),
                pltpu.VMEM(w_rev.shape, bf16),
                pltpu.VMEM(w_down.shape, bf16),
                pltpu.VMEM(w_atom.shape, bf16),
                pltpu.VMEM((n_atoms, width), f32),
                pltpu.VMEM((n_src, own, depth), bf16),
                pltpu.VMEM((n_src, own, depth), bf16),
                dma((n_dst,)),
                dma((10,)),
                dma((n_src,)),
                dma((n_src,)),
                dma((n_dst,)),
                dma((n_dst,)),
                dma((n_src,)),
                dma((n_src,)),
            ],
            compiler_params=pltpu.CompilerParams(
                collective_id=0, has_side_effects=True, vmem_limit_bytes=VMEM_MIB * 2**20
            ),
        )(
            edge_in, atom_in, targets.reshape(n_dst, 1, RB), reverse.reshape(n_dst, 1, RB), counts.reshape(n_dst),
            w_in, gains, w_layers, w_rev, w_down, w_atom,
        )

    both = ("src", "dst")
    in_specs = (
        P(both, None), P(("dst", "src"), None), P(both), P(both), P("src", "dst", None),
        P(), P(), P(), P(), P(), P(),
    )
    out_specs = (P(both, None), P(("dst", "src"), None))
    return jax.shard_map(on_device, mesh=mesh, in_specs=in_specs, out_specs=out_specs, check_vma=False)
```

time: 133 us -> 121 us (0.910)
  the two profiles are of different devices: /device:TPU:57 before, /device:TPU:32 now
where the time goes in v2:
time: 121 us
  Pallas kernels  118 us (98%)
  local copies, waits for them, and re-layouts  2.63 us (2%)
    pallas_call x1, Pallas kernels, on_device(): pl.pallas_call(functools.partial(kernel, n_src, n_dst), out_shape=(pltpu....  118 us
    unnamed x2, local copies, waits for them, and re-layouts  2.63 us

profile of v2, /device:TPU:32, one launch (start us, length us, event | category | flops | bytes accessed | tf_op | source)
XLA Modules:
  0.0 121.1 jit_solution(15882611398959304371)
XLA Ops:
  0.6 117.8 %shard_map.122 = (bf16[4096,512]{1,0:T(8,128)(2,1)S(1)}, bf16[64,256]{1,0:T(8,128)(2,1)S(1)}) custom-call(bf16[4096,512]{1,0:T(8,128)(2,1)} %edge_ref.1, bf16[64,256]{1,0:T(8,128)(2,1)} %atom_ref.1, s32[32,1,128]{2,1,0:T(1,128)} %bitcast.3, s32[32,1,128]{2,1,0:T(1,128)} %bitcast.4, s32[32]{0:T(128)} %bitcast.5, bf16[256,512]{1,0:T(8,128)(2,1)} %w_in_ref.1, ...), custom_call_target="tpu_custom_call" | custom-call | tf_op jit(solution)/shard_map/pallas_call | solution.py:248
  118.5 2.0 %copy.15 = bf16[4096,512]{1,0:T(8,128)(2,1)} copy(bf16[4096,512]{1,0:T(8,128)(2,1)S(1)} %get-tuple-element.2) | data formatting | bytes 8388608
  120.5 0.6 copy.16

commit v3 on v2

--- a/solution.py
+++ b/solution.py
@@ -13,6 +13,7 @@
 AHEAD = 2
 BEHIND = 2
 VMEM_MIB = 54
+EARLY = (2, 4)
 
 
 def silu(v):
@@ -33,7 +34,8 @@
     edge_ref, atom_ref, targ_ref, rev_ref, cnt_ref, w_in_ref, gains_ref, w_lay_ref, w_rev_ref, w_down_ref, w_atom_ref,
     edge_out_ref, atom_out_ref,
     edges, xs, send, recv, atoms, proj, targ, rev, cnt, gains, w_in, w_lay, w_rev, w_down, w_atom, seg, part, parts,
-    in_sem, w_sem, at_send, at_recv, send_sem, recv_sem, pt_send, pt_recv,
+    rows_send, rows_recv,
+    in_sem, w_sem, at_send, at_recv, send_sem, recv_sem, pt_send, pt_recv, rw_send, rw_recv,
 ):
     planes = n_dst // PLANE
     width = edges.shape[1]
@@ -88,6 +90,41 @@
     loads[0].wait()
     pl.semaphore_wait(barrier, n_src + n_dst - 2)
 
+    def block_copy(k):
+        return pltpu.make_async_remote_copy(
+            src_ref=send.at[k], dst_ref=recv.at[me], send_sem=send_sem.at[k], recv_sem=recv_sem.at[me],
+            device_id={"dst": k}, device_id_type=MESH,
+        )
+
+    def arrival(k):
+        return pltpu.make_async_remote_copy(
+            src_ref=send.at[k], dst_ref=recv.at[k], send_sem=send_sem.at[k], recv_sem=recv_sem.at[k],
+            device_id={"dst": k}, device_id_type=MESH,
+        )
+
+    def own_copy():
+        return pltpu.make_async_copy(send.at[me], recv.at[me], recv_sem.at[me])
+
+    def rows_copy(s):
+        return pltpu.make_async_remote_copy(
+            src_ref=rows_send.at[s], dst_ref=rows_recv.at[s], send_sem=rw_send.at[s], recv_sem=rw_recv.at[s],
+            device_id={"dst": partner(EARLY[s], 1)}, device_id_type=MESH,
+        )
+
+    def early(n):
+        return functools.reduce(jnp.logical_or, [n == e for e in EARLY])
+
+    def reorder(k):
+        sub = lax.broadcasted_iota(jnp.int32, (RB, RB), 0)
+        return (sub == rev[k]).astype(jnp.float32).astype(jnp.bfloat16)
+
+    def edge_layers(x):
+        for layer in range(layers):
+            scale = lax.rsqrt(jnp.mean(x * x, axis=-1, keepdims=True) + 1e-6)
+            normed = (x * scale * gains[layer : layer + 1, :]).astype(jnp.bfloat16)
+            x = x + silu(jnp.dot(normed, w_lay[layer], preferred_element_type=jnp.float32))
+        return x
+
     def atom_copy(d):
         return pltpu.make_async_remote_copy(
             src_ref=atoms.at[row], dst_ref=atoms.at[row], send_sem=at_send.at[d], recv_sem=at_recv.at[d],
@@ -108,6 +145,13 @@
     for load in loads[1:6]:
         load.wait()
 
+    for n in EARLY:
+        k = partner(n, 1)
+        edge_load(k).wait()
+        moved = jnp.dot(reorder(k), edges[rows_of(k), :], preferred_element_type=jnp.float32)
+        send[k] = moved.astype(jnp.bfloat16)
+        block_copy(k).start()
+
     @pl.loop(1, n_src)
     def _(d):
         atom_arrival(d).wait_recv()
@@ -116,30 +160,22 @@
     def _(d):
         atom_copy(d).wait_send()
 
-    whole = atoms[...].reshape(n_atoms, atoms.shape[2])
-    proj[...] = jnp.dot(whole, w_in[...], preferred_element_type=jnp.float32).astype(jnp.bfloat16)
-
-    def block_copy(k):
-        return pltpu.make_async_remote_copy(
-            src_ref=send.at[k], dst_ref=recv.at[me], send_sem=send_sem.at[k], recv_sem=recv_sem.at[me],
-            device_id={"dst": k}, device_id_type=MESH,
-        )
-
-    def arrival(k):
-        return pltpu.make_async_remote_copy(
-            src_ref=send.at[k], dst_ref=recv.at[k], send_sem=send_sem.at[k], recv_sem=recv_sem.at[k],
-            device_id={"dst": k}, device_id_type=MESH,
-        )
-
-    def own_copy():
-        return pltpu.make_async_copy(send.at[me], recv.at[me], recv_sem.at[me])
+    def every_atom():
+        return atoms[...].reshape(n_atoms, atoms.shape[2])
+
+    proj[...] = jnp.dot(every_atom(), w_in[...], preferred_element_type=jnp.float32).astype(jnp.bfloat16)
 
     @pl.loop(0, n_dst // AHEAD)
     def _(step):
-        ks = [partner(step * AHEAD + g, 1) for g in range(AHEAD)]
+        ns = [step * AHEAD + g for g in range(AHEAD)]
+        ks = [partner(n, 1) for n in ns]
         hot, base = [], []
-        for k in ks:
-            edge_load(k).wait()
+        for n, k in zip(ns, ks):
+
+            @pl.when(jnp.logical_not(early(n)))
+            def _():
+                edge_load(k).wait()
+
             base.append(edges[rows_of(k), :].astype(jnp.float32))
             col = jnp.broadcast_to(targ[k], (RB, RB)).T
             lane = lax.broadcasted_iota(jnp.int32, (RB, RB), 1)
@@ -149,36 +185,55 @@
                 )
             )
         picked = jnp.dot(jnp.concatenate(hot, axis=0), proj[...], preferred_element_type=jnp.float32)
-        x = jnp.concatenate(base, axis=0) + picked
-        for layer in range(layers):
-            scale = lax.rsqrt(jnp.mean(x * x, axis=-1, keepdims=True) + 1e-6)
-            normed = (x * scale * gains[layer : layer + 1, :]).astype(jnp.bfloat16)
-            x = x + silu(jnp.dot(normed, w_lay[layer], preferred_element_type=jnp.float32))
+        x = edge_layers(jnp.concatenate(base, axis=0) + picked)
         sent = x.astype(jnp.bfloat16)
-        for g, k in enumerate(ks):
+        for g, (n, k) in enumerate(zip(ns, ks)):
             xs[rows_of(k), :] = x[g * RB : (g + 1) * RB, :]
-            sub = lax.broadcasted_iota(jnp.int32, (RB, RB), 0)
-            perm = (sub == rev[k]).astype(jnp.float32).astype(jnp.bfloat16)
-            moved = jnp.dot(perm, sent[g * RB : (g + 1) * RB, :], preferred_element_type=jnp.float32)
-            send[k] = moved.astype(jnp.bfloat16)
-
-            @pl.when(k != me)
-            def _():
-                block_copy(k).start()
-
-            @pl.when(k == me)
-            def _():
-                own_copy().start()
+            perm = reorder(k)
+
+            def whole_rows():
+                moved = jnp.dot(perm, sent[g * RB : (g + 1) * RB, :], preferred_element_type=jnp.float32)
+                send[k] = moved.astype(jnp.bfloat16)
+
+                @pl.when(k != me)
+                def _():
+                    block_copy(k).start()
+
+                @pl.when(k == me)
+                def _():
+                    own_copy().start()
+
+            def atom_rows(s):
+                rows = jnp.dot(hot[g], every_atom(), preferred_element_type=jnp.float32).astype(jnp.bfloat16)
+                rows_send[s] = jnp.dot(perm, rows, preferred_element_type=jnp.float32).astype(jnp.bfloat16)
+                rows_copy(s).start()
+
+            pl.when(jnp.logical_not(early(n)))(whole_rows)
+            for s, e in enumerate(EARLY):
+                if e % AHEAD == g:
+                    pl.when(n == e)(functools.partial(atom_rows, s))
 
     for load in loads[6:]:
         load.wait()
 
+    begun = []
+    for s, n in enumerate(EARLY):
+        k = partner(n, -1)
+        arrival(k).wait_recv()
+        rows_copy(s).wait_recv()
+        near = jnp.dot(rows_recv[s], w_in[...], preferred_element_type=jnp.float32).astype(jnp.bfloat16)
+        begun.append(recv[k].astype(jnp.float32) + near.astype(jnp.float32))
+    states = edge_layers(jnp.concatenate(begun, axis=0)).astype(jnp.bfloat16)
+    for s, n in enumerate(EARLY):
+        recv[partner(n, -1)] = states[s * RB : (s + 1) * RB, :]
+
     @pl.loop(0, n_dst // BEHIND)
     def _(step):
-        ks = [partner(step * BEHIND + g, -1) for g in range(BEHIND)]
-        for k in ks:
-
-            @pl.when(k != me)
+        ns = [step * BEHIND + g for g in range(BEHIND)]
+        ks = [partner(n, -1) for n in ns]
+        for n, k in zip(ns, ks):
+
+            @pl.when((k != me) & jnp.logical_not(early(n)))
             def _():
                 arrival(k).wait_recv()
 
@@ -232,6 +287,9 @@
         @pl.when(k != me)
         def _():
             arrival(k).wait_send()
+
+    for s in range(len(EARLY)):
+        rows_copy(s).wait_send()
 
 
 def solution(mesh):
@@ -272,6 +330,8 @@
                 pltpu.VMEM((n_atoms, width), f32),
                 pltpu.VMEM((n_src, own, depth), bf16),
                 pltpu.VMEM((n_src, own, depth), bf16),
+                pltpu.VMEM((len(EARLY), RB, depth), bf16),
+                pltpu.VMEM((len(EARLY), RB, depth), bf16),
                 dma((n_dst,)),
                 dma((10,)),
                 dma((n_src,)),
@@ -280,6 +340,8 @@
                 dma((n_dst,)),
                 dma((n_src,)),
                 dma((n_src,)),
+                dma((len(EARLY),)),
+                dma((len(EARLY),)),
             ],
             compiler_params=pltpu.CompilerParams(
                 collective_id=0, has_side_effects=True, vmem_limit_bytes=VMEM_MIB * 2**20

time: 121 us -> 119 us (0.983)
  Pallas kernels: 118 us -> 116 us
    pallas_call x1, Pallas kernels: 118 us -> 116 us  [on_device(): pl.pallas_call(functools.partial(kernel, n_src, n_dst), out_shape=(pltpu....]
where the time goes in v3:
time: 119 us
  Pallas kernels  116 us (97%)
  local copies, waits for them, and re-layouts  2.63 us (2%)
    pallas_call x1, Pallas kernels, on_device(): pl.pallas_call(functools.partial(kernel, n_src, n_dst), out_shape=(pltpu....  116 us
    unnamed x2, local copies, waits for them, and re-layouts  2.63 us

profile of v3, /device:TPU:32, one launch (start us, length us, event | category | flops | bytes accessed | tf_op | source)
XLA Modules:
  0.0 119.4 jit_solution(5569635307579655089)
XLA Ops:
  0.6 116.1 %shard_map.122 = (bf16[4096,512]{1,0:T(8,128)(2,1)S(1)}, bf16[64,256]{1,0:T(8,128)(2,1)S(1)}) custom-call(bf16[4096,512]{1,0:T(8,128)(2,1)} %edge_ref.1, bf16[64,256]{1,0:T(8,128)(2,1)} %atom_ref.1, s32[32,1,128]{2,1,0:T(1,128)} %bitcast.3, s32[32,1,128]{2,1,0:T(1,128)} %bitcast.4, s32[32]{0:T(128)} %bitcast.5, bf16[256,512]{1,0:T(8,128)(2,1)} %w_in_ref.1, ...), custom_call_target="tpu_custom_call" | custom-call | tf_op jit(solution)/shard_map/pallas_call | solution.py:306
  116.8 2.0 %copy.15 = bf16[4096,512]{1,0:T(8,128)(2,1)} copy(bf16[4096,512]{1,0:T(8,128)(2,1)S(1)} %get-tuple-element.2) | data formatting | bytes 8388608
  118.8 0.6 copy.16

commit v4 on v3

--- a/solution.py
+++ b/solution.py
@@ -57,6 +57,7 @@
 
     def partner(n, way):
         r, i = n // PLANE, lax.rem(n, PLANE)
+        r = jnp.where(r >= planes - 2, 2 * planes - 3 - r, r)
         dz = planes // 2 * lax.rem(r + i, 2) + lax.rem(r // 2 + i + 1, planes // 2)
         py = lax.rem(y + i, 2)
         pc = lax.rem(c + (i + 1) // 2, 2)
@@ -87,36 +88,45 @@
     for load in loads[6:]:
         load.start()
     seg[...] = jnp.zeros_like(seg)
-    loads[0].wait()
-    pl.semaphore_wait(barrier, n_src + n_dst - 2)
-
-    def block_copy(k):
-        return pltpu.make_async_remote_copy(
-            src_ref=send.at[k], dst_ref=recv.at[me], send_sem=send_sem.at[k], recv_sem=recv_sem.at[me],
-            device_id={"dst": k}, device_id_type=MESH,
-        )
-
-    def arrival(k):
-        return pltpu.make_async_remote_copy(
-            src_ref=send.at[k], dst_ref=recv.at[k], send_sem=send_sem.at[k], recv_sem=recv_sem.at[k],
-            device_id={"dst": k}, device_id_type=MESH,
-        )
-
-    def own_copy():
-        return pltpu.make_async_copy(send.at[me], recv.at[me], recv_sem.at[me])
-
-    def rows_copy(s):
-        return pltpu.make_async_remote_copy(
-            src_ref=rows_send.at[s], dst_ref=rows_recv.at[s], send_sem=rw_send.at[s], recv_sem=rw_recv.at[s],
-            device_id={"dst": partner(EARLY[s], 1)}, device_id_type=MESH,
-        )
-
-    def early(n):
-        return functools.reduce(jnp.logical_or, [n == e for e in EARLY])
 
     def reorder(k):
         sub = lax.broadcasted_iota(jnp.int32, (RB, RB), 0)
         return (sub == rev[k]).astype(jnp.float32).astype(jnp.bfloat16)
+
+    for load in loads[1:6]:
+        load.wait()
+    for n in EARLY:
+        k = partner(n, 1)
+        edge_load(k).wait()
+        moved = jnp.dot(reorder(k), edges[rows_of(k), :], preferred_element_type=jnp.float32)
+        send[k] = moved.astype(jnp.bfloat16)
+
+    loads[0].wait()
+    pl.semaphore_wait(barrier, n_src + n_dst - 2)
+
+    def block_copy(k):
+        return pltpu.make_async_remote_copy(
+            src_ref=send.at[k], dst_ref=recv.at[me], send_sem=send_sem.at[k], recv_sem=recv_sem.at[me],
+            device_id={"dst": k}, device_id_type=MESH,
+        )
+
+    def arrival(k):
+        return pltpu.make_async_remote_copy(
+            src_ref=send.at[k], dst_ref=recv.at[k], send_sem=send_sem.at[k], recv_sem=recv_sem.at[k],
+            device_id={"dst": k}, device_id_type=MESH,
+        )
+
+    def own_copy():
+        return pltpu.make_async_copy(send.at[me], recv.at[me], recv_sem.at[me])
+
+    def rows_copy(s):
+        return pltpu.make_async_remote_copy(
+            src_ref=rows_send.at[s], dst_ref=rows_recv.at[s], send_sem=rw_send.at[s], recv_sem=rw_recv.at[s],
+            device_id={"dst": partner(EARLY[s], 1)}, device_id_type=MESH,
+        )
+
+    def early(n):
+        return functools.reduce(jnp.logical_or, [n == e for e in EARLY])
 
     def edge_layers(x):
         for layer in range(layers):
@@ -138,19 +148,12 @@
             device_id={"src": sender}, device_id_type=MESH,
         )
 
+    for n in EARLY:
+        block_copy(partner(n, 1)).start()
+
     @pl.loop(1, n_src)
     def _(d):
         atom_copy(d).start()
-
-    for load in loads[1:6]:
-        load.wait()
-
-    for n in EARLY:
-        k = partner(n, 1)
-        edge_load(k).wait()
-        moved = jnp.dot(reorder(k), edges[rows_of(k), :], preferred_element_type=jnp.float32)
-        send[k] = moved.astype(jnp.bfloat16)
-        block_copy(k).start()
 
     @pl.loop(1, n_src)
     def _(d):

time: 119 us -> 120 us (level); the launches traced: 119 us -> 118 us
  Pallas kernels: 116 us -> 114 us
    pallas_call x1, Pallas kernels: 116 us -> 114 us  [on_device(): pl.pallas_call(functools.partial(kernel, n_src, n_dst), out_shape=(pltpu....]
where the time goes in v4:
time: 120 us; the launch traced here: 118 us
  Pallas kernels  114 us (95%)
  local copies, waits for them, and re-layouts  2.63 us (2%)
    pallas_call x1, Pallas kernels, on_device(): pl.pallas_call(functools.partial(kernel, n_src, n_dst), out_shape=(pltpu....  114 us
    unnamed x2, local copies, waits for them, and re-layouts  2.63 us

profile of v4, /device:TPU:32, one launch (start us, length us, event | category | flops | bytes accessed | tf_op | source)
XLA Modules:
  0.0 117.8 jit_solution(13939869341029040167)
XLA Ops:
  0.6 114.5 %shard_map.122 = (bf16[4096,512]{1,0:T(8,128)(2,1)S(1)}, bf16[64,256]{1,0:T(8,128)(2,1)S(1)}) custom-call(bf16[4096,512]{1,0:T(8,128)(2,1)} %edge_ref.1, bf16[64,256]{1,0:T(8,128)(2,1)} %atom_ref.1, s32[32,1,128]{2,1,0:T(1,128)} %bitcast.3, s32[32,1,128]{2,1,0:T(1,128)} %bitcast.4, s32[32]{0:T(128)} %bitcast.5, bf16[256,512]{1,0:T(8,128)(2,1)} %w_in_ref.1, ...), custom_call_target="tpu_custom_call" | custom-call | tf_op jit(solution)/shard_map/pallas_call | solution.py:309
  115.1 2.0 %copy.15 = bf16[4096,512]{1,0:T(8,128)(2,1)} copy(bf16[4096,512]{1,0:T(8,128)(2,1)S(1)} %get-tuple-element.2) | data formatting | bytes 8388608
  117.2 0.6 copy.16

commit v5 on v3

--- a/solution.py
+++ b/solution.py
@@ -57,6 +57,7 @@
 
     def partner(n, way):
         r, i = n // PLANE, lax.rem(n, PLANE)
+        r = jnp.where(r >= planes - 2, 2 * planes - 3 - r, r)
         dz = planes // 2 * lax.rem(r + i, 2) + lax.rem(r // 2 + i + 1, planes // 2)
         py = lax.rem(y + i, 2)
         pc = lax.rem(c + (i + 1) // 2, 2)

time: 119 us -> 119 us (level); the launches traced: 119 us -> 118 us
    pallas_call x1, Pallas kernels: 116 us -> 115 us  [on_device(): pl.pallas_call(functools.partial(kernel, n_src, n_dst), out_shape=(pltpu....]
where the time goes in v5:
time: 119 us; the launch traced here: 118 us
  Pallas kernels  115 us (97%)
  local copies, waits for them, and re-layouts  2.63 us (2%)
    pallas_call x1, Pallas kernels, on_device(): pl.pallas_call(functools.partial(kernel, n_src, n_dst), out_shape=(pltpu....  115 us
    unnamed x2, local copies, waits for them, and re-layouts  2.63 us

profile of v5, /device:TPU:32, one launch (start us, length us, event | category | flops | bytes accessed | tf_op | source)
XLA Modules:
  0.0 118.1 jit_solution(15172416532779818894)
XLA Ops:
  0.6 114.8 %shard_map.122 = (bf16[4096,512]{1,0:T(8,128)(2,1)S(1)}, bf16[64,256]{1,0:T(8,128)(2,1)S(1)}) custom-call(bf16[4096,512]{1,0:T(8,128)(2,1)} %edge_ref.1, bf16[64,256]{1,0:T(8,128)(2,1)} %atom_ref.1, s32[32,1,128]{2,1,0:T(1,128)} %bitcast.3, s32[32,1,128]{2,1,0:T(1,128)} %bitcast.4, s32[32]{0:T(128)} %bitcast.5, bf16[256,512]{1,0:T(8,128)(2,1)} %w_in_ref.1, ...), custom_call_target="tpu_custom_call" | custom-call | tf_op jit(solution)/shard_map/pallas_call | solution.py:307
  115.5 2.0 %copy.15 = bf16[4096,512]{1,0:T(8,128)(2,1)} copy(bf16[4096,512]{1,0:T(8,128)(2,1)S(1)} %get-tuple-element.2) | data formatting | bytes 8388608
  117.5 0.6 copy.16
